TPU v7x, 256 devices: a whole 4x4x8 slice. The times are simulated.
256 devices in a mesh: dp: 128 (over x, y, z), group: 2 (over core).
Axes of the slice: x: 4, y: 4, z: 8, core: 2. Of those that a mesh axis runs over, the one named last changes fastest.
Arguments:
- features: bfloat16 [32768, 32768], P(('dp', 'group')), may hold values from -6 to 6
- grad_slab: float32 [32768, 64], P('dp'), may hold values from -6 to 6
- damping: float32 [128], replicated, may hold values from 0.05 to 0.5
- owner_of: int32 [128], replicated, may hold values from 0 to 127, each once
Outputs:
- preconditioned: bfloat16 [32768, 64], replicated
Inputs may be any that keep to these rules, and one draw needn't show every extreme that they name: `owner_of`: each dp index owns exactly one block.
All inputs are finite; a program needn't handle non-finite values. Where the computation divides by a largest or mean magnitude, that divisor is 1e-20 or more.
Results may differ from a plain program's by a relative error of at most 0.0004.
Values may be sent and summed in bfloat16 or wider, within the bound.
A program may use at most 128 MiB of HBM per device.

v0:
```python
import jax
import jax.numpy as jnp
from jax import lax
from jax.sharding import PartitionSpec as P

B = 256
ITERS = 3


def shards(features, grad_slab, damping, owner_of):
    hi = lax.Precision.HIGHEST
    rows = features.shape[0]
    owners = lax.axis_size("dp")
    cores = lax.axis_size("group")
    total = rows * owners * cores
    myself = lax.axis_index("dp")
    core = lax.axis_index("group")
    slots = jnp.arange(owners, dtype=jnp.int32)
    slot_block = jnp.sum(jnp.where(owner_of[None, :] == slots[:, None], slots[None, :], 0), axis=1)
    blocks = features.reshape(rows, owners, B)
    ordered = jnp.take(blocks, slot_block, axis=1)
    arrived = lax.all_to_all(ordered, "dp", split_axis=1, concat_axis=0, tiled=True)
    arrived = arrived.reshape(rows * owners, B)
    partial_value = lax.dot_general(
        arrived, arrived, (((0,), (0,)), ((), ())), preferred_element_type=jnp.float32
    )
    cov = lax.psum(partial_value, "group") / total
    eye = jnp.eye(B, dtype=jnp.float32)
    mine = slot_block[myself]
    mat = cov + damping[mine] * eye
    alpha = 1.0 / jnp.max(jnp.sum(jnp.abs(mat), axis=1))
    inverse = alpha * eye
    half = B // 2
    for step in range(ITERS):
        columns = lax.dynamic_slice_in_dim(inverse, core * half, half, 1)
        fresh = 2.0 * columns - jnp.dot(inverse, jnp.dot(mat, columns, precision=hi), precision=hi)
        inverse = lax.all_gather(fresh, "group", axis=1, tiled=True)
    my_rows = lax.dynamic_slice_in_dim(inverse, core * half, half, 0)
    product = jnp.dot(my_rows, grad_slab, precision=hi).astype(jnp.bfloat16)
    gathered = lax.all_gather(product, ("dp", "group"), axis=0, tiled=True)
    by_owner = gathered.reshape(owners, B, gathered.shape[1])
    by_block = jnp.take(by_owner, owner_of, axis=0)
    return by_block.reshape(owners * B, gathered.shape[1])


def solution(mesh):
    return jax.shard_map(
        shards,
        mesh=mesh,
        in_specs=(P(("dp", "group"), None), P("dp", None), P(), P()),
        out_specs=P(),
        check_vma=False,
    )
```

profile of v0, /device:TPU:1, one launch (start us, length us, event | category | flops | bytes accessed | tf_op | source)
XLA Modules:
  0.0 419.5 jit_solution(17723180424688873971)
XLA Ops:
  6.5 0.8 select_reduce_fusion
  7.4 11.9 %copy.13 = bf16[128,32768]{0,1:T(8,128)(2,1)} copy(bf16[128,32768]{1,0:T(8,128)(2,1)} %param.4) | data formatting | bytes 16777216 | tf_op args[0]
  19.3 11.9 %copy.14 = bf16[128,128,256]{2,0,1:T(8,128)(2,1)} copy(bf16[128,128,256]{0,2,1:T(8,128)(2,1)} %bitcast.35) | data formatting | bytes 16777216 | tf_op jit(solution)/shard_map/reshape | solution.py:20
  31.2 9.9 %gather_fusion = bf16[128,128,256]{2,1,0:T(8,128)(2,1)} fusion(bf16[128,128,256]{2,0,1:T(8,128)(2,1)} %copy.14, s32[1024]{0:T(1024)S(1)} %pad_clamp_fusion.1), kind=kCustom, calls=%fused_computation | custom fusion | bytes 16777728 | tf_op jit(solution)/shard_map/jit(_take)/gather | solution.py:21
  41.1 7.4 %select_bitcast_fusion = bf16[128,128,256]{2,0,1:T(8,128)(2,1)} fusion(bf16[128,128,256]{2,1,0:T(8,128)(2,1)} %gather_fusion, pred[128]{0:T(512)(128)(4,1)S(1)} %compare_and_fusion), kind=kLoop, calls=%fused_computation.4 | loop fusion | flops 4194304 | bytes 16777344 | tf_op jit(solution)/shard_map/jit(_take)/select_n | solution.py:21
  48.5 203.2 %all_to_all.15 = bf16[128,128,256]{2,0,1:T(8,128)(2,1)S(1)} all-to-all(bf16[128,128,256]{2,0,1:T(8,128)(2,1)} %select_bitcast_fusion), channel_id=1, replica_groups=mesh['dp'=128,'group'=2] {'dp'}, dimensions={1} | all-to-all | bytes 16777216 | tf_op jit(solution)/shard_map/all_to_all | solution.py:22
  251.7 3.1 fusion.2
  254.9 0.6 dynamic_slice.18
  257.4 0.6 dynamic_slice.19
  258.0 21.2 %all-reduce.2.cloned.1.call-done = f32[256,256]{1,0:T(8,128)} async-done(((f32[256,256]{1,0:T(8,128)}), f32[256,256]{1,0:T(8,128)}) %all-reduce.2.cloned.1.call-update) | async-done | bytes 262160 | tf_op jit(solution)/shard_map/psum | solution.py:27
  279.3 1.7 abs_reduce_fusion
  281.0 0.6 reduce_max.9
  282.3 2.0 fusion.11
  284.6 2.0 all_gather.12
  286.6 2.0 fusion.9
  289.0 2.0 all_gather.13
  291.0 1.9 fusion.7
  293.3 2.0 all_gather.14
  295.3 0.9 convolution_convert_fusion
  296.4 101.2 %all-gather.2.cloned.1.call-done = bf16[32768,64]{0,1:T(8,128)(2,1)} async-done(((bf16[128,64]{0,1:T(8,128)(2,1)}), bf16[32768,64]{0,1:T(8,128)(2,1)}) %all-gather.2.cloned.1.call-update) | async-done | bytes 4194320 | tf_op jit(solution)/shard_map/all_gather | solution.py:40
  397.6 4.8 %copy.22 = bf16[8,128,8,256]{3,2,0,1:T(8,128)(2,1)} copy(bf16[8,128,8,256]{3,2,1,0:T(8,128)(2,1)} %bitcast.37) | data formatting | bytes 8388608 | tf_op jit(solution)/shard_map/reshape | solution.py:41
  402.4 4.9 %gather_fusion.1 = bf16[128,256,64]{1,2,0:T(8,128)(2,1)} fusion(bf16[128,256,64]{1,2,0:T(8,128)(2,1)} %bitcast.33, s32[1024]{0:T(1024)S(1)} %pad_clamp_fusion), kind=kCustom, calls=%fused_computation.1 | custom fusion | bytes 8389120 | tf_op jit(solution)/shard_map/jit(_take)/gather | solution.py:42
  407.3 2.5 copy.20
  409.8 2.9 broadcast_select_fusion
  (22 shorter events, 1.4 us)
Async XLA Ops:
  6.5 288.8 %copy-start = (f32[256,64]{0,1:T(8,128)S(1)}, f32[256,64]{0,1:T(8,128)}, u32[]{:S(2)}) copy-start(f32[256,64]{0,1:T(8,128)} %param.5) | copy-start | bytes 196612
  6.5 272.7 %all-reduce.2.cloned.1.call-start = ((), (), s32[]{:S(2)}) async-start(), calls=%async_computation.1 | async-start | bytes 524288 | tf_op jit(solution)/shard_map/psum | solution.py:27
  251.7 5.7 %copy-start.1 = (f32[128]{0:T(128)S(1)}, f32[128]{0:T(128)}, u32[]{:S(2)}) copy-start(f32[128]{0:T(128)} %param.6) | copy-start | bytes 1540
  251.7 44.5 %copy-start.2 = (s32[128]{0:T(128)S(1)}, s32[128]{0:T(128)}, u32[]{:S(2)}) copy-start(s32[128]{0:T(128)} %param.7) | copy-start | bytes 1540
  254.8 142.8 %all-gather.2.cloned.1.call-start = ((), (), s32[]{:S(2)}) async-start(), calls=%async_computation.2 | async-start | bytes 4210688 | tf_op jit(solution)/shard_map/all_gather | solution.py:40
Sparse Core Ops, SparseCore 0:
  254.9 24.2 all-reduce.1
  296.3 101.2 all-gather.1
where the time goes:
time: 421 us; the launch traced here: 420 us
  blocking collectives  209 us (50%)
  waiting for transfers between devices  122 us (29%)
  local copies, waits for them, and re-layouts  47.3 us (11%)
  between operations  16.1 us (4%)
  other arithmetic  13.4 us (3%)
  matrix products  10.9 us (3%)
    all_to_all x1, blocking collectives, shards(): lax.all_to_all(ordered, 'dp', split_axis=1, concat_axis=0, tiled=True)  203 us
    all_gather x1, waiting for transfers between devices, shards(): gathered = lax.all_gather(product, ('dp', 'group'), axis=0, tiled=True)  101 us
    psum x1, waiting for transfers between devices, shards(): cov = lax.psum(partial_value, 'group') / total  21.2 us
    reshape x1, local copies, waits for them, and re-layouts, shards(): blocks = features.reshape(rows, owners, B)  11.9 us
    unnamed x7, local copies, waits for them, and re-layouts  11.9 us
    gather x1, local copies, waits for them, and re-layouts, shards(): ordered = jnp.take(blocks, slot_block, axis=1)  9.95 us
  transfers between devices with their start and end apart: 2, of which 2 were waited for; matrix products, arithmetic and copies ran while one was open for 0% of the time, Pallas kernels for 0%

commit v1 on v0

v1 whole, which is shorter than its diff:
```python
import jax
import jax.numpy as jnp
from jax import lax
from jax.experimental import pallas as pl
from jax.experimental.pallas import tpu as pltpu
from jax.sharding import PartitionSpec as P

B = 256
H = B // 2
COLS = 64
TOTAL = 32768
NX, NY, NZ = 4, 4, 8
NK = NZ // 2
OWNERS = NX * NY * NZ
ROWS = 128
HA = 64
HB = 72
F32 = jnp.float32
BF16 = jnp.bfloat16
MESH = pl.DeviceIdType.MESH


def order(i):
    return jnp.where(i == 0, 2, jnp.where(i == 3, 0, 2 * i - 1))


def dp_index(x, y, z):
    return (x * NY + y) * NZ + z


def reduce_kernel(
    slot_block, damping, features, slab_t, gathered,
    feat, xs, xr, pa, pb, tra, trb, pla, plb, sma, smb,
    l2sa, l2sb, l2ra, l2rb, l3s, l3r,
    feat_sem, ex_s, ex_r, l1_s, l1_r, l2_s, l2_r, l3_ss, l3_rs,
    ag1_s, ag1_r, ag2_s, ag3_s, ag_r, fw_s, fw_r,
):
    dp = lax.axis_index("dp")
    c = lax.axis_index("group")
    x = dp // (NY * NZ)
    y = (dp // NZ) % NY
    z = dp % NZ

    def load(b, carry):
        pltpu.make_async_copy(features.at[:, pl.ds(pl.multiple_of(b * B, B), B)], feat.at[b], feat_sem).start()
        return carry

    lax.fori_loop(0, OWNERS, load, 0)

    def at(xx, yy, zz, cc):
        return (dp_index(xx, yy, zz), cc)

    sibling = (dp, 1 - c)
    xnb = [at((x + d) % NX, y, z, c) for d in range(NX)]
    ynb = [at(x, (y + d) % NY, z, c) for d in range(NY)]
    znb = [at(x, y, (z + d) % NZ, c) for d in range(NZ)]

    barrier = pltpu.get_barrier_semaphore()
    peers = [sibling] + xnb[1:] + ynb[1:] + znb[1:]
    for peer in peers:
        pl.semaphore_signal(barrier, inc=1, device_id=peer, device_id_type=MESH)
    pl.semaphore_wait(barrier, len(peers))

    def remote(src, dst, s, r, dev):
        return pltpu.make_async_remote_copy(
            src_ref=src, dst_ref=dst, send_sem=s, recv_sem=r, device_id=dev, device_id_type=MESH
        )

    pltpu.make_async_copy(feat, feat, feat_sem).wait()

    def slot_of(dx, dy, k, cc):
        return dp_index((x + dx) % NX, (y + dy) % NY, 2 * k + cc)

    def block_of(dx, dy, k, cc):
        return feat[slot_block[slot_of(dx, dy, k, cc)]]

    def exchange(g, carry):
        dx, dy = order(g // 4), order(g % 4)
        for k in range(NK):
            xs[g, k] = block_of(dx, dy, k, 1 - c)
        remote(xs.at[g], xr.at[g], ex_s.at[g], ex_r.at[g], sibling).start()
        return carry

    lax.fori_loop(0, 16, exchange, 0)

    row = lax.broadcasted_iota(jnp.int32, (H, H), 0)
    col = lax.broadcasted_iota(jnp.int32, (H, H), 1)

    def level1(kind, axis, way, t):
        s, r = l1_s.at[kind, axis, way, t], l1_r.at[kind, axis, way, t]
        if axis == 0:
            src = {(0, 0): pa.at[2, t, 0], (0, 1): pa.at[2, t, 1], (1, 0): pa.at[1, t, 1], (1, 1): pa.at[3, t, 0],
                   (2, 0): pa.at[1, t, 0], (2, 1): pa.at[3, t, 1]}[kind, way]
            dst = (tra, pla, sma)[kind].at[way, t]
            dev = xnb[1 if way == 0 else 3]
        else:
            src = {(0, 0): pb.at[t, 2, 0], (0, 1): pb.at[t, 2, 1], (1, 0): pb.at[t, 1, 1], (1, 1): pb.at[t, 3, 0],
                   (2, 0): pb.at[t, 1, 0], (2, 1): pb.at[t, 3, 1]}[kind, way]
            dst = (trb, plb, smb)[kind].at[way, t]
            dev = ynb[1 if way == 0 else 3]
        return remote(src, dst, s, r, dev)

    def group(g, carry):
        dx, dy = order(g // 4), order(g % 4)
        remote(xs.at[g], xr.at[g], ex_s.at[g], ex_r.at[g], sibling).wait_recv()

        def slot(k, inner):
            own = block_of(dx, dy, k, c)
            f = jnp.concatenate([own, xr[g, k]], axis=0)
            t = lax.dot_general(f, f, (((0,), (0,)), ((), ())), preferred_element_type=F32)
            t00, t01, t11 = t[:H, :H], t[:H, H:], t[H:, H:]
            pa[dx, dy, 0, k] = t01[:HA]
            pa[dx, dy, 1, k] = t01[HA:]
            both = jnp.where(row < col, t00, t11)
            on = row == col
            d0 = jnp.sum(jnp.where(on, t00, 0.0), axis=0, keepdims=True)
            d1 = jnp.sum(jnp.where(on, t11, 0.0), axis=0, keepdims=True)
            pb[dx, dy, 0, k, :HA] = both[:HA]
            pb[dx, dy, 0, k, HA:] = jnp.broadcast_to(d0, (HB - HA, H))
            pb[dx, dy, 1, k, :HA] = both[HA:]
            pb[dx, dy, 1, k, HA:] = jnp.broadcast_to(d1, (HB - HA, H))
            return inner

        lax.fori_loop(0, NK, slot, 0)
        for axis, d, t in ((0, dx, dy), (1, dy, dx)):
            @pl.when(d == 2)
            def _():
                level1(0, axis, 0, t).start()
                level1(0, axis, 1, t).start()

            @pl.when(d == 1)
            def _():
                level1(1, axis, 0, t).start()

            @pl.when(d == 3)
            def _():
                level1(1, axis, 1, t).start()
        return carry

    lax.fori_loop(0, 16, group, 0)

    def pass_on(i, carry):
        t = order(i)
        for axis, p, tr in ((0, pa, tra), (1, pb, trb)):
            for way, d in ((0, 1), (1, 3)):
                level1(0, axis, way, t).wait_recv()
                ref = p.at[d, t, way] if axis == 0 else p.at[t, d, way]
                ref[...] = ref[...] + tr[way, t]
                level1(2, axis, way, t).start()
        return carry

    lax.fori_loop(0, 4, pass_on, 0)

    def level2(part, d):
        s, r = l2_s.at[part, d], l2_r.at[part, d]
        if part == 0:
            return remote(l2sa.at[d], l2ra.at[d], s, r, at(x, (y + d) % NY, z, c))
        return remote(l2sb.at[d], l2rb.at[d], s, r, at((x + d) % NX, y, z, c))

    def finish1(i, carry):
        t = order(i)
        for axis, p, plain, sums, out in ((0, pa, pla, sma, l2sa), (1, pb, plb, smb, l2sb)):
            for way in (0, 1):
                level1(1, axis, way, t).wait_recv()
                level1(2, axis, way, t).wait_recv()
            own = p.at[0, t] if axis == 0 else p.at[t, 0]
            out[t, 0] = own[0] + sums[0, t] + plain[1, t]
            out[t, 1] = own[1] + sums[1, t] + plain[0, t]

            @pl.when(t != 0)
            def _():
                level2(axis, t).start()
        return carry

    lax.fori_loop(0, 4, finish1, 0)

    for part, out, got, lo, size in ((0, l2sa, l2ra, 0, HA), (1, l2sb, l2rb, 2 * HA, HB)):
        for d in (1, 3, 2):
            level2(part, d).wait_recv()
        for h in (0, 1):
            l3s[:, lo + h * size : lo + (h + 1) * size] = out[0, h] + got[1, h] + got[2, h] + got[3, h]

    def level3(k):
        d = (2 * k + c - z + NZ) % NZ
        return remote(l3s.at[k], l3r.at[d], l3_ss.at[k], l3_rs.at[d], at(x, y, 2 * k + c, c))

    for k in range(NK):
        @pl.when(2 * k + c != z)
        def _():
            level3(k).start()

    owner = z % 2 == c
    xy = x * NY + y
    kz = z // 2

    def ag1(d):
        return remote(gathered.at[c, xy, kz], gathered.at[c, xy, kz], ag1_s.at[d], ag1_r.at[kz], znb[d])

    @pl.when(owner)
    def _():
        for d in range(1, NZ):
            pltpu.make_async_remote_copy(
                src_ref=l3r.at[d], dst_ref=l3r.at[d], send_sem=l3_ss.at[0], recv_sem=l3_rs.at[d],
                device_id=znb[d], device_id_type=MESH,
            ).wait_recv()
        total = l3s[kz]
        for d in range(1, NZ):
            total = total + l3r[d]
        scale = 1.0 / TOTAL
        t01 = total[: 2 * HA] * scale
        both = jnp.concatenate([total[2 * HA : 3 * HA], total[2 * HA + HB : 3 * HA + HB]], axis=0) * scale
        damp = damping[slot_block[dp]]
        d0 = total[3 * HA : 3 * HA + 1] * scale + damp
        d1 = total[3 * HA + HB : 3 * HA + HB + 1] * scale + damp
        flip = both.T
        t00 = jnp.where(row < col, both, jnp.where(row > col, flip, d0))
        t11 = jnp.where(row > col, both, jnp.where(row < col, flip, d1))
        mat = jnp.concatenate(
            [jnp.concatenate([t00, t01], axis=1), jnp.concatenate([t01.T, t11], axis=1)], axis=0
        )
        alpha = 1.0 / jnp.max(jnp.sum(jnp.abs(mat), axis=0, keepdims=True), axis=1, keepdims=True)

        def times(v):
            return jnp.dot(v, mat, precision=lax.Precision.HIGHEST, preferred_element_type=F32)

        def first(v):
            return 2.0 * alpha * v - alpha * alpha * times(v)

        def second(v):
            p = first(v)
            return 2.0 * p - first(times(p))

        v = second(slab_t[...])
        result = 2.0 * v - second(times(v))
        gathered[c, xy, kz] = result.astype(BF16)
        for d in range(1, NZ):
            ag1(d).start()

    for k in range(NK):
        @pl.when(2 * k + c != z)
        def _():
            pltpu.make_async_remote_copy(
                src_ref=gathered.at[c, xy, k], dst_ref=gathered.at[c, xy, k], send_sem=ag1_s.at[0], recv_sem=ag1_r.at[k],
                device_id=sibling, device_id_type=MESH,
            ).wait_recv()

    def bundle(cc, h, q):
        return gathered.at[cc, q, pl.ds(2 * h, 2)]

    def line(h, d):
        return x * NY + (y + d) % NY if h == 0 else ((x + d) % NX) * NY + y

    def ag2(h, d):
        dev = ynb[d] if h == 0 else xnb[d]
        return remote(bundle(c, h, xy), bundle(c, h, xy), ag2_s.at[h, d], ag_r.at[h, xy], dev)

    def ag3(h, e, d):
        q = line(h, e)
        dev = xnb[d] if h == 0 else ynb[d]
        return remote(bundle(c, h, q), bundle(c, h, q), ag3_s.at[h, e, d], ag_r.at[h, q], dev)

    def landed(h, q):
        remote(bundle(c, h, q), bundle(c, h, q), ag2_s.at[0, 0], ag_r.at[h, q], sibling).wait_recv()

    def forward(cc, h, q):
        return remote(bundle(cc, h, q), bundle(cc, h, q), fw_s.at[h, q], fw_r.at[h, q], sibling)

    for h in (0, 1):
        for d in (2, 1, 3):
            ag2(h, d).start()
    for h in (0, 1):
        for d in (2, 1, 3):
            ag3(h, 0, d).start()
        forward(c, h, xy).start()
    for e in (1, 3, 2):
        for h in (0, 1):
            landed(h, line(h, e))
            for d in (2, 1, 3):
                ag3(h, e, d).start()
            forward(c, h, line(h, e)).start()
    for e in (0, 1, 3, 2):
        for d in (1, 3, 2):
            for h in (0, 1):
                ex, ey = (d, e) if h == 0 else (e, d)
                q = ((x + ex) % NX) * NY + (y + ey) % NY
                landed(h, q)
                forward(c, h, q).start()

    def sent_exchange(g, carry):
        remote(xs.at[g], xr.at[g], ex_s.at[g], ex_r.at[g], sibling).wait_send()
        return carry

    lax.fori_loop(0, 16, sent_exchange, 0)

    def sent_level1(t, carry):
        for kind in range(3):
            for axis in (0, 1):
                for way in (0, 1):
                    level1(kind, axis, way, t).wait_send()
        return carry

    lax.fori_loop(0, 4, sent_level1, 0)
    for part in (0, 1):
        for d in (1, 2, 3):
            level2(part, d).wait_send()
    for k in range(NK):
        @pl.when(2 * k + c != z)
        def _():
            level3(k).wait_send()

    @pl.when(owner)
    def _():
        for d in range(1, NZ):
            ag1(d).wait_send()

    for h in (0, 1):
        for d in (1, 2, 3):
            ag2(h, d).wait_send()
            for e in range(4):
                ag3(h, e, d).wait_send()

    def sent_forward(q, carry):
        for h in (0, 1):
            forward(c, h, q).wait_send()
            forward(1 - c, h, q).wait_recv()
        return carry

    lax.fori_loop(0, 16, sent_forward, 0)


def permute_kernel(owner_of, gathered, out):
    def one(b, carry):
        o = owner_of[b]
        q, z = o // NZ, o % NZ
        out[:, pl.ds(pl.multiple_of(b * B, B), B)] = gathered[z % 2, q, z // 2]
        return carry

    lax.fori_loop(0, OWNERS, one, 0, unroll=4)


def shards(features, grad_slab, damping, owner_of):
    slots = jnp.arange(OWNERS, dtype=jnp.int32)
    slot_block = jnp.sum(jnp.where(owner_of[None, :] == slots[:, None], slots[None, :], 0), axis=1)
    vmem = pl.BlockSpec(memory_space=pltpu.VMEM)
    smem = pl.BlockSpec(memory_space=pltpu.SMEM)
    dma = pltpu.SemaphoreType.DMA
    gathered = pl.pallas_call(
        reduce_kernel,
        out_shape=jax.ShapeDtypeStruct((2, NX * NY, NK, COLS, B), BF16),
        in_specs=[smem, smem, pl.BlockSpec(memory_space=pl.ANY), vmem],
        out_specs=vmem,
        scratch_shapes=[
            pltpu.VMEM((OWNERS, ROWS, B), BF16),
            pltpu.VMEM((16, NK, ROWS, B), BF16),
            pltpu.VMEM((16, NK, ROWS, B), BF16),
            pltpu.VMEM((4, 4, 2, NK, HA, H), F32),
            pltpu.VMEM((4, 4, 2, NK, HB, H), F32),
            *[pltpu.VMEM((2, 4, NK, rows, H), F32) for _ in range(3) for rows in (HA, HB)],
            pltpu.VMEM((4, 2, NK, HA, H), F32),
            pltpu.VMEM((4, 2, NK, HB, H), F32),
            pltpu.VMEM((4, 2, NK, HA, H), F32),
            pltpu.VMEM((4, 2, NK, HB, H), F32),
            pltpu.VMEM((NK, 2 * (HA + HB), H), F32),
            pltpu.VMEM((NZ, 2 * (HA + HB), H), F32),
            dma,
            dma((16,)), dma((16,)),
            dma((3, 2, 2, 4)), dma((3, 2, 2, 4)),
            dma((2, 4)), dma((2, 4)),
            dma((NK,)), dma((NZ,)),
            dma((NZ,)), dma((NK,)),
            dma((2, 4)), dma((2, 4, 4)), dma((2, 16)),
            dma((2, 16)), dma((2, 16)),
        ],
        compiler_params=pltpu.CompilerParams(
            collective_id=0, has_side_effects=True, vmem_limit_bytes=58 * 1024 * 1024
        ),
    )(slot_block, damping, features, grad_slab.T)
    out = pl.pallas_call(
        permute_kernel,
        out_shape=jax.ShapeDtypeStruct((COLS, OWNERS * B), BF16),
        in_specs=[smem, vmem],
        out_specs=vmem,
        compiler_params=pltpu.CompilerParams(vmem_limit_bytes=32 * 1024 * 1024),
    )(owner_of, gathered)
    return out.T


def solution(mesh):
    return jax.shard_map(
        shards,
        mesh=mesh,
        in_specs=(P(("dp", "group"), None), P("dp", None), P(), P()),
        out_specs=P(),
        check_vma=False,
    )
```

time: 421 us -> 120 us (0.29)
  blocking collectives: 209 us -> 0 us
  waiting for transfers between devices: 122 us -> 0 us
  Pallas kernels: 0 us -> 117 us
  local copies, waits for them, and re-layouts: 47.3 us -> 2.18 us
  between operations: 16.1 us -> 0.03 us
  other arithmetic: 13.4 us -> 1.28 us
  matrix products: 10.9 us -> 0 us
    all_to_all x1 -> x0, blocking collectives: 203 us -> none  [shards(): lax.all_to_all(ordered, 'dp', split_axis=1, concat_axis=0, tiled=True)]
    pallas_call x0 -> x2, Pallas kernels: none -> 117 us  [the longest x1 112 us: shards(): pl.pallas_call(reduce_kernel, out_shape=jax.ShapeDtypeStruct((2, NX * NY,...]
    all_gather x1 -> x0, waiting for transfers between devices: 101 us -> none  [shards(): gathered = lax.all_gather(product, ('dp', 'group'), axis=0, tiled=True)]
    psum x1 -> x0, waiting for transfers between devices: 21.2 us -> none  [shards(): cov = lax.psum(partial_value, 'group') / total]
    gather x3 -> x0, local copies, waits for them, and re-layouts: 17.3 us -> none  [the longest x1 9.95 us: shards(): ordered = jnp.take(blocks, slot_block, axis=1)]
    reshape x2 -> x0, local copies, waits for them, and re-layouts: 16.7 us -> none  [the longest x1 11.9 us: shards(): blocks = features.reshape(rows, owners, B)]
    dot_general x8 -> x0, matrix products: 10.9 us -> none  [the longest x3 5.85 us: shards(): jnp.dot(mat, columns, precision=hi)]
    select_n x4 -> x0, other arithmetic: 10.3 us -> none  [the longest x2 7.41 us: shards(): ordered = jnp.take(blocks, slot_block, axis=1)]
  transfers between devices with their start and end apart: 2 -> 0, of which waited for: 2 -> 0; matrix products, arithmetic and copies ran while one was open for 0% -> 0% of each run, Pallas kernels for 0% -> 0%
where the time goes in v1:
time: 120 us
  Pallas kernels  117 us (98%)
  local copies, waits for them, and re-layouts  2.18 us (2%)
  other arithmetic  1.28 us (1%)
    pallas_call x1, Pallas kernels, shards(): pl.pallas_call(reduce_kernel, out_shape=jax.ShapeDtypeStruct((2, NX * NY,...  112 us
    pallas_call x1, Pallas kernels, shards(): pl.pallas_call(permute_kernel, out_shape=jax.ShapeDtypeStruct((COLS, OWNE...  4.56 us

profile of v1, /device:TPU:1, one launch (start us, length us, event | category | flops | bytes accessed | tf_op | source)
XLA Modules:
  0.0 120.2 jit_solution(14715045129276046161)
XLA Ops:
  0.0 1.3 %select_reduce_fusion.slot_block = s32[128]{0:T(128)} fusion(s32[128]{0:T(128)} %owner_of.1), kind=kLoop, calls=%fused_computation | loop fusion | flops 49024 | bytes 1024 | tf_op jit(solution)/shard_map/reduce_sum | solution.py:343
  1.3 0.0 copy-start.1
  1.3 112.1 %shard_map.46.gathered = bf16[2,16,4,64,256]{4,3,2,1,0:T(8,128)(2,1)} custom-call(s32[128]{0:T(128)} %select_reduce_fusion.slot_block, f32[128]{0:T(128)} %damping.1, bf16[128,32768]{1,0:T(8,128)(2,1)} %features.1, f32[64,256]{1,0:T(8,128)} %bitcast.2), custom_call_target="tpu_custom_call" | custom-call | tf_op jit(solution)/shard_map/pallas_call | solution.py:347
  113.4 0.0 copy-done.1
  113.4 0.0 copy-start
  113.5 2.2 %copy-done = bf16[2,16,4,64,256]{4,3,2,1,0:T(8,128)(2,1)S(1)} copy-done((bf16[2,16,4,64,256]{4,3,2,1,0:T(8,128)(2,1)S(1)}, bf16[2,16,4,64,256]{4,3,2,1,0:T(8,128)(2,1)}, u32[]{:S(2)}) %copy-start) | copy-done | bytes 4194328
  115.6 4.6 %shard_map.47 = bf16[64,32768]{1,0:T(8,128)(2,1)} custom-call(s32[128]{0:T(128)S(1)} %copy-done.1, bf16[2,16,4,64,256]{4,3,2,1,0:T(8,128)(2,1)S(1)} %copy-done), custom_call_target="tpu_custom_call" | custom-call | tf_op jit(solution)/shard_map/pallas_call | solution.py:378
Async XLA Ops:
  1.3 112.2 %copy-start.1 = (s32[128]{0:T(128)S(1)}, s32[128]{0:T(128)}, u32[]{:S(2)}) copy-start(s32[128]{0:T(128)} %owner_of.1) | copy-start | bytes 1540
  113.4 2.2 %copy-start = (bf16[2,16,4,64,256]{4,3,2,1,0:T(8,128)(2,1)S(1)}, bf16[2,16,4,64,256]{4,3,2,1,0:T(8,128)(2,1)}, u32[]{:S(2)}) copy-start(bf16[2,16,4,64,256]{4,3,2,1,0:T(8,128)(2,1)} %shard_map.46.gathered) | copy-start | bytes 12582916

commit v2 on v1

--- a/solution.py
+++ b/solution.py
@@ -15,6 +15,7 @@
 ROWS = 128
 HA = 64
 HB = 72
+CODED = 4 * HA + 16
 F32 = jnp.float32
 BF16 = jnp.bfloat16
 MESH = pl.DeviceIdType.MESH
@@ -28,10 +29,38 @@
     return (x * NY + y) * NZ + z
 
 
+def encode(ref, parts, diagonals, tokens):
+    unit = tokens // 512
+    line = lax.broadcasted_iota(jnp.int32, (16, H), 0)
+    extra = jnp.zeros((16, H), F32)
+    for i, v in enumerate(parts):
+        top = jnp.max(jnp.abs(v), axis=0, keepdims=True)
+        units = jnp.maximum(jnp.ceil(top * (1.0 / unit)), 1.0)
+        coded = jnp.round(v * ((32767.0 / unit) / units))
+        ref[HA * i : HA * (i + 1)] = coded.astype(jnp.int32).astype(jnp.int16)
+        extra = jnp.where(line == i, units, extra)
+    for i, d in diagonals.items():
+        scaled = d * (32767.0 / (36.0 * tokens))
+        high = jnp.floor(scaled)
+        low = jnp.round((scaled - high) * 32767.0)
+        extra = jnp.where(line == 4 + i, high, jnp.where(line == 8 + i, low, extra))
+    ref[4 * HA :] = extra.astype(jnp.int32).astype(jnp.int16)
+
+
+def decode(ref, tokens):
+    unit = tokens // 512
+    extra = ref[4 * HA :].astype(jnp.int32).astype(F32)
+    parts = []
+    for i in range(4):
+        v = ref[HA * i : HA * (i + 1)].astype(jnp.int32).astype(F32)
+        parts.append(v * (extra[i : i + 1] * (unit / 32767.0)))
+    rows = (extra[4:8] + extra[8:12] * (1.0 / 32767.0)) * (36.0 * tokens / 32767.0)
+    return parts, [rows[i : i + 1] for i in range(4)]
+
+
 def reduce_kernel(
     slot_block, damping, features, slab_t, gathered,
-    feat, xs, xr, pa, pb, tra, trb, pla, plb, sma, smb,
-    l2sa, l2sb, l2ra, l2rb, l3s, l3r,
+    feat, xs, xr, pa, pb, sent1, got1, sent2, got2, sent3, got3,
     feat_sem, ex_s, ex_r, l1_s, l1_r, l2_s, l2_r, l3_ss, l3_rs,
     ag1_s, ag1_r, ag2_s, ag3_s, ag_r, fw_s, fw_r,
 ):
@@ -59,8 +88,6 @@
     peers = [sibling] + xnb[1:] + ynb[1:] + znb[1:]
     for peer in peers:
         pl.semaphore_signal(barrier, inc=1, device_id=peer, device_id_type=MESH)
-    pl.semaphore_wait(barrier, len(peers))
-
     def remote(src, dst, s, r, dev):
         return pltpu.make_async_remote_copy(
             src_ref=src, dst_ref=dst, send_sem=s, recv_sem=r, device_id=dev, device_id_type=MESH
@@ -74,10 +101,15 @@
     def block_of(dx, dy, k, cc):
         return feat[slot_block[slot_of(dx, dy, k, cc)]]
 
+    def stage(g, carry):
+        for k in range(NK):
+            xs[g, k] = block_of(order(g // 4), order(g % 4), k, 1 - c)
+        return carry
+
+    lax.fori_loop(0, 16, stage, 0)
+    pl.semaphore_wait(barrier, len(peers))
+
     def exchange(g, carry):
-        dx, dy = order(g // 4), order(g % 4)
-        for k in range(NK):
-            xs[g, k] = block_of(dx, dy, k, 1 - c)
         remote(xs.at[g], xr.at[g], ex_s.at[g], ex_r.at[g], sibling).start()
         return carry
 
@@ -87,107 +119,128 @@
     col = lax.broadcasted_iota(jnp.int32, (H, H), 1)
 
     def level1(kind, axis, way, t):
-        s, r = l1_s.at[kind, axis, way, t], l1_r.at[kind, axis, way, t]
-        if axis == 0:
-            src = {(0, 0): pa.at[2, t, 0], (0, 1): pa.at[2, t, 1], (1, 0): pa.at[1, t, 1], (1, 1): pa.at[3, t, 0],
-                   (2, 0): pa.at[1, t, 0], (2, 1): pa.at[3, t, 1]}[kind, way]
-            dst = (tra, pla, sma)[kind].at[way, t]
-            dev = xnb[1 if way == 0 else 3]
-        else:
-            src = {(0, 0): pb.at[t, 2, 0], (0, 1): pb.at[t, 2, 1], (1, 0): pb.at[t, 1, 1], (1, 1): pb.at[t, 3, 0],
-                   (2, 0): pb.at[t, 1, 0], (2, 1): pb.at[t, 3, 1]}[kind, way]
-            dst = (trb, plb, smb)[kind].at[way, t]
-            dev = ynb[1 if way == 0 else 3]
-        return remote(src, dst, s, r, dev)
+        dev = (xnb, ynb)[axis][1 if way == 0 else 3]
+        return remote(
+            sent1.at[kind, axis, way, t], got1.at[kind, axis, way, t],
+            l1_s.at[kind, axis, way, t], l1_r.at[kind, axis, way, t], dev,
+        )
+
+    def place(part, d, t):
+        return pa.at[d, t] if part == 0 else pb.at[t, d]
+
+    def pieces(ref, part, half):
+        parts = [ref[half, k, :HA] for k in range(NK)]
+        return parts, ({k: ref[half, k, HA : HA + 1] for k in range(NK)} if part == 1 else {})
+
+    def send1(kind, part, d, half, way, t):
+        parts, diagonals = pieces(place(part, d, t), part, half)
+        encode(sent1.at[kind, part, way, t], parts, diagonals, 512)
+        level1(kind, part, way, t).start()
 
     def group(g, carry):
         dx, dy = order(g // 4), order(g % 4)
         remote(xs.at[g], xr.at[g], ex_s.at[g], ex_r.at[g], sibling).wait_recv()
 
-        def slot(k, inner):
+        for k in range(NK):
             own = block_of(dx, dy, k, c)
             f = jnp.concatenate([own, xr[g, k]], axis=0)
             t = lax.dot_general(f, f, (((0,), (0,)), ((), ())), preferred_element_type=F32)
             t00, t01, t11 = t[:H, :H], t[:H, H:], t[H:, H:]
             pa[dx, dy, 0, k] = t01[:HA]
             pa[dx, dy, 1, k] = t01[HA:]
-            both = jnp.where(row < col, t00, t11)
             on = row == col
+            both = jnp.where(row < col, t00, jnp.where(on, 0.0, t11))
             d0 = jnp.sum(jnp.where(on, t00, 0.0), axis=0, keepdims=True)
             d1 = jnp.sum(jnp.where(on, t11, 0.0), axis=0, keepdims=True)
             pb[dx, dy, 0, k, :HA] = both[:HA]
             pb[dx, dy, 0, k, HA:] = jnp.broadcast_to(d0, (HB - HA, H))
             pb[dx, dy, 1, k, :HA] = both[HA:]
             pb[dx, dy, 1, k, HA:] = jnp.broadcast_to(d1, (HB - HA, H))
-            return inner
-
-        lax.fori_loop(0, NK, slot, 0)
-        for axis, d, t in ((0, dx, dy), (1, dy, dx)):
+
+        for part, d, t in ((0, dx, dy), (1, dy, dx)):
             @pl.when(d == 2)
             def _():
-                level1(0, axis, 0, t).start()
-                level1(0, axis, 1, t).start()
+                send1(0, part, 2, 0, 0, t)
+                send1(0, part, 2, 1, 1, t)
 
             @pl.when(d == 1)
             def _():
-                level1(1, axis, 0, t).start()
+                send1(1, part, 1, 1, 0, t)
 
             @pl.when(d == 3)
             def _():
-                level1(1, axis, 1, t).start()
+                send1(1, part, 3, 0, 1, t)
         return carry
 
     lax.fori_loop(0, 16, group, 0)
 
     def pass_on(i, carry):
         t = order(i)
-        for axis, p, tr in ((0, pa, tra), (1, pb, trb)):
+        for part in (0, 1):
             for way, d in ((0, 1), (1, 3)):
-                level1(0, axis, way, t).wait_recv()
-                ref = p.at[d, t, way] if axis == 0 else p.at[t, d, way]
-                ref[...] = ref[...] + tr[way, t]
-                level1(2, axis, way, t).start()
+                level1(0, part, way, t).wait_recv()
+                parts, rows = decode(got1.at[0, part, way, t], 512)
+                own, diagonals = pieces(place(part, d, t), part, way)
+                parts = [a + b for a, b in zip(own, parts)]
+                diagonals = {k: diagonals[k] + rows[k] for k in diagonals}
+                encode(sent1.at[2, part, way, t], parts, diagonals, 512)
+                level1(2, part, way, t).start()
         return carry
 
     lax.fori_loop(0, 4, pass_on, 0)
 
+    def add_coded(ref, part, half, coded, tokens):
+        for message in coded:
+            parts, rows = decode(message, tokens)
+            for k in range(NK):
+                ref[half, k, :HA] = ref[half, k, :HA] + parts[k]
+                if part == 1:
+                    ref[half, k, HA:] = ref[half, k, HA:] + rows[k]
+
     def level2(part, d):
-        s, r = l2_s.at[part, d], l2_r.at[part, d]
-        if part == 0:
-            return remote(l2sa.at[d], l2ra.at[d], s, r, at(x, (y + d) % NY, z, c))
-        return remote(l2sb.at[d], l2rb.at[d], s, r, at((x + d) % NX, y, z, c))
+        dev = at(x, (y + d) % NY, z, c) if part == 0 else at((x + d) % NX, y, z, c)
+        return remote(sent2.at[part, d], got2.at[part, d], l2_s.at[part, d], l2_r.at[part, d], dev)
 
     def finish1(i, carry):
         t = order(i)
-        for axis, p, plain, sums, out in ((0, pa, pla, sma, l2sa), (1, pb, plb, smb, l2sb)):
+        for part in (0, 1):
             for way in (0, 1):
-                level1(1, axis, way, t).wait_recv()
-                level1(2, axis, way, t).wait_recv()
-            own = p.at[0, t] if axis == 0 else p.at[t, 0]
-            out[t, 0] = own[0] + sums[0, t] + plain[1, t]
-            out[t, 1] = own[1] + sums[1, t] + plain[0, t]
+                level1(1, part, way, t).wait_recv()
+                level1(2, part, way, t).wait_recv()
+            ref = place(part, 0, t)
+            for half in (0, 1):
+                add_coded(ref, part, half, (got1.at[2, part, half, t], got1.at[1, part, 1 - half, t]), 512)
 
             @pl.when(t != 0)
             def _():
-                level2(axis, t).start()
+                for half in (0, 1):
+                    encode(sent2.at[part, t, half], *pieces(ref, part, half), 1024)
+                level2(part, t).start()
         return carry
 
     lax.fori_loop(0, 4, finish1, 0)
 
-    for part, out, got, lo, size in ((0, l2sa, l2ra, 0, HA), (1, l2sb, l2rb, 2 * HA, HB)):
+    for part in (0, 1):
         for d in (1, 3, 2):
             level2(part, d).wait_recv()
-        for h in (0, 1):
-            l3s[:, lo + h * size : lo + (h + 1) * size] = out[0, h] + got[1, h] + got[2, h] + got[3, h]
+            for half in (0, 1):
+                add_coded(place(part, 0, 0), part, half, (got2.at[part, d, half],), 1024)
 
     def level3(k):
         d = (2 * k + c - z + NZ) % NZ
-        return remote(l3s.at[k], l3r.at[d], l3_ss.at[k], l3_rs.at[d], at(x, y, 2 * k + c, c))
-
-    for k in range(NK):
+        return remote(sent3.at[k], got3.at[d], l3_ss.at[k], l3_rs.at[d], at(x, y, 2 * k + c, c))
+
+    def send3(k, carry):
         @pl.when(2 * k + c != z)
         def _():
+            parts = [pa[0, 0, 0, k], pa[0, 0, 1, k], pb[0, 0, 0, k, :HA], pb[0, 0, 1, k, :HA]]
+            diagonals = {2: pb[0, 0, 0, k, HA : HA + 1], 3: pb[0, 0, 1, k, HA : HA + 1]}
+            encode(sent3.at[k], parts, diagonals, 4096)
             level3(k).start()
+
+        return carry
+
+    lax.fori_loop(0, NK, send3, 0)
 
     owner = z % 2 == c
     xy = x * NY + y
@@ -198,20 +251,20 @@
 
     @pl.when(owner)
     def _():
-        for d in range(1, NZ):
-            pltpu.make_async_remote_copy(
-                src_ref=l3r.at[d], dst_ref=l3r.at[d], send_sem=l3_ss.at[0], recv_sem=l3_rs.at[d],
-                device_id=znb[d], device_id_type=MESH,
-            ).wait_recv()
-        total = l3s[kz]
-        for d in range(1, NZ):
-            total = total + l3r[d]
+        t01a, t01b = pa[0, 0, 0, kz], pa[0, 0, 1, kz]
+        ba, bb = pb[0, 0, 0, kz, :HA], pb[0, 0, 1, kz, :HA]
+        d0, d1 = pb[0, 0, 0, kz, HA : HA + 1], pb[0, 0, 1, kz, HA : HA + 1]
+        for d in (1, 7, 2, 6, 3, 5, 4):
+            remote(got3.at[d], got3.at[d], l3_ss.at[0], l3_rs.at[d], znb[d]).wait_recv()
+            parts, rows = decode(got3.at[d], 4096)
+            t01a, t01b, ba, bb = t01a + parts[0], t01b + parts[1], ba + parts[2], bb + parts[3]
+            d0, d1 = d0 + rows[2], d1 + rows[3]
         scale = 1.0 / TOTAL
-        t01 = total[: 2 * HA] * scale
-        both = jnp.concatenate([total[2 * HA : 3 * HA], total[2 * HA + HB : 3 * HA + HB]], axis=0) * scale
+        t01 = jnp.concatenate([t01a, t01b], axis=0) * scale
+        both = jnp.concatenate([ba, bb], axis=0) * scale
         damp = damping[slot_block[dp]]
-        d0 = total[3 * HA : 3 * HA + 1] * scale + damp
-        d1 = total[3 * HA + HB : 3 * HA + HB + 1] * scale + damp
+        d0 = d0 * scale + damp
+        d1 = d1 * scale + damp
         flip = both.T
         t00 = jnp.where(row < col, both, jnp.where(row > col, flip, d0))
         t11 = jnp.where(row > col, both, jnp.where(row < col, flip, d1))
@@ -328,14 +381,17 @@
     lax.fori_loop(0, 16, sent_forward, 0)
 
 
-def permute_kernel(owner_of, gathered, out):
+def permute_kernel(owner_of, gathered, out, sem):
     def one(b, carry):
         o = owner_of[b]
         q, z = o // NZ, o % NZ
-        out[:, pl.ds(pl.multiple_of(b * B, B), B)] = gathered[z % 2, q, z // 2]
-        return carry
-
-    lax.fori_loop(0, OWNERS, one, 0, unroll=4)
+        pltpu.make_async_copy(
+            gathered.at[z % 2, q, z // 2], out.at[:, pl.ds(pl.multiple_of(b * B, B), B)], sem
+        ).start()
+        return carry
+
+    lax.fori_loop(0, OWNERS, one, 0, unroll=8)
+    pltpu.make_async_copy(out, out, sem).wait()
 
 
 def shards(features, grad_slab, damping, owner_of):
@@ -346,7 +402,7 @@
     dma = pltpu.SemaphoreType.DMA
     gathered = pl.pallas_call(
         reduce_kernel,
-        out_shape=jax.ShapeDtypeStruct((2, NX * NY, NK, COLS, B), BF16),
+        out_shape=pltpu.VMEM((2, NX * NY, NK, COLS, B), BF16),
         in_specs=[smem, smem, pl.BlockSpec(memory_space=pl.ANY), vmem],
         out_specs=vmem,
         scratch_shapes=[
@@ -355,13 +411,12 @@
             pltpu.VMEM((16, NK, ROWS, B), BF16),
             pltpu.VMEM((4, 4, 2, NK, HA, H), F32),
             pltpu.VMEM((4, 4, 2, NK, HB, H), F32),
-            *[pltpu.VMEM((2, 4, NK, rows, H), F32) for _ in range(3) for rows in (HA, HB)],
-            pltpu.VMEM((4, 2, NK, HA, H), F32),
-            pltpu.VMEM((4, 2, NK, HB, H), F32),
-            pltpu.VMEM((4, 2, NK, HA, H), F32),
-            pltpu.VMEM((4, 2, NK, HB, H), F32),
-            pltpu.VMEM((NK, 2 * (HA + HB), H), F32),
-            pltpu.VMEM((NZ, 2 * (HA + HB), H), F32),
+            pltpu.VMEM((3, 2, 2, 4, CODED, H), jnp.int16),
+            pltpu.VMEM((3, 2, 2, 4, CODED, H), jnp.int16),
+            pltpu.VMEM((2, 4, 2, CODED, H), jnp.int16),
+            pltpu.VMEM((2, 4, 2, CODED, H), jnp.int16),
+            pltpu.VMEM((NK, CODED, H), jnp.int16),
+            pltpu.VMEM((NZ, CODED, H), jnp.int16),
             dma,
             dma((16,)), dma((16,)),
             dma((3, 2, 2, 4)), dma((3, 2, 2, 4)),
@@ -379,7 +434,8 @@
         permute_kernel,
         out_shape=jax.ShapeDtypeStruct((COLS, OWNERS * B), BF16),
         in_specs=[smem, vmem],
-        out_specs=vmem,
+        out_specs=pl.BlockSpec(memory_space=pl.ANY),
+        scratch_shapes=[dma],
         compiler_params=pltpu.CompilerParams(vmem_limit_bytes=32 * 1024 * 1024),
     )(owner_of, gathered)
     return out.T

time: 120 us -> 81.6 us (0.68)
  Pallas kernels: 117 us -> 80.1 us
  local copies, waits for them, and re-layouts: 2.18 us -> 0.01 us
    pallas_call x1, Pallas kernels: 112 us -> 77.1 us  [shards(): pl.pallas_call(reduce_kernel, out_shape=pltpu.VMEM((2, NX * NY, NK, COLS,...]
    unnamed x4 -> x2, local copies, waits for them, and re-layouts: 2.18 us -> 0.01 us
    pallas_call x1, Pallas kernels: 4.56 us -> 3.04 us  [shards(): pl.pallas_call(permute_kernel, out_shape=jax.ShapeDtypeStruct((COLS, OWNE...]
where the time goes in v2:
time: 81.6 us; the launch traced here: 81.4 us
  Pallas kernels  80.1 us (98%)
  other arithmetic  1.28 us (2%)
    pallas_call x1, Pallas kernels, shards(): pl.pallas_call(reduce_kernel, out_shape=pltpu.VMEM((2, NX * NY, NK, COLS,...  77.1 us
    pallas_call x1, Pallas kernels, shards(): pl.pallas_call(permute_kernel, out_shape=jax.ShapeDtypeStruct((COLS, OWNE...  3.04 us

profile of v2, /device:TPU:1, one launch (start us, length us, event | category | flops | bytes accessed | tf_op | source)
XLA Modules:
  0.0 81.4 jit_solution(1886164129959275622)
XLA Ops:
  0.0 1.3 %select_reduce_fusion.slot_block = s32[128]{0:T(128)} fusion(s32[128]{0:T(128)} %owner_of.1), kind=kLoop, calls=%fused_computation | loop fusion | flops 49024 | bytes 1024 | tf_op jit(solution)/shard_map/reduce_sum | solution.py:399
  1.3 0.0 copy-start
  1.3 77.1 %shard_map.46.gathered = bf16[2,16,4,64,256]{4,3,2,1,0:T(8,128)(2,1)S(1)} custom-call(s32[128]{0:T(128)} %select_reduce_fusion.slot_block, f32[128]{0:T(128)} %damping.1, bf16[128,32768]{1,0:T(8,128)(2,1)} %features.1, f32[64,256]{1,0:T(8,128)} %bitcast.2), custom_call_target="tpu_custom_call" | custom-call | tf_op jit(solution)/shard_map/pallas_call | solution.py:403
  78.4 0.0 copy-done
  78.4 3.0 %shard_map.47 = bf16[64,32768]{1,0:T(8,128)(2,1)} custom-call(s32[128]{0:T(128)S(1)} %copy-done, bf16[2,16,4,64,256]{4,3,2,1,0:T(8,128)(2,1)S(1)} %shard_map.46.gathered), custom_call_target="tpu_custom_call" | custom-call | tf_op jit(solution)/shard_map/pallas_call | solution.py:433
Async XLA Ops:
  1.3 77.1 %copy-start = (s32[128]{0:T(128)S(1)}, s32[128]{0:T(128)}, u32[]{:S(2)}) copy-start(s32[128]{0:T(128)} %owner_of.1) | copy-start | bytes 1540

commit v3 on v2

--- a/solution.py
+++ b/solution.py
@@ -13,6 +13,7 @@
 NK = NZ // 2
 OWNERS = NX * NY * NZ
 ROWS = 128
+AHEAD = 3
 HA = 64
 HB = 72
 CODED = 4 * HA + 16
@@ -23,6 +24,19 @@
 
 def order(i):
     return jnp.where(i == 0, 2, jnp.where(i == 3, 0, 2 * i - 1))
+
+
+def pick(g):
+    r = jnp.maximum(g - 7, 0)
+    even = g % 2 == 0
+    dx = jnp.where(g < 7, jnp.where(even, 2, order((g + 1) // 2)), order(1 + r // 3))
+    dy = jnp.where(g < 7, jnp.where(even, order(g // 2), 2), order(1 + r % 3))
+    return dx, dy
+
+
+def rank(z, c, k):
+    away = (k - (z - c + NZ) // 2 % NK + NK) % NK
+    return away + away // 2 - 2 * (away // 3)
 
 
 def dp_index(x, y, z):
@@ -59,9 +73,9 @@
 
 
 def reduce_kernel(
-    slot_block, damping, features, slab_t, gathered,
-    feat, xs, xr, pa, pb, sent1, got1, sent2, got2, sent3, got3,
-    feat_sem, ex_s, ex_r, l1_s, l1_r, l2_s, l2_r, l3_ss, l3_rs,
+    owner_of, damping_in, features, slab_in, gathered,
+    slot_block, damping, slab_t, table, feat, xs, xr, pa, pb, sent1, got1, sent2, got2, sent3, got3,
+    small_sem, feat_sem, ex_s, ex_r, l1_s, l1_r, l2_s, l2_r, l3_ss, l3_rs,
     ag1_s, ag1_r, ag2_s, ag3_s, ag_r, fw_s, fw_r,
 ):
     dp = lax.axis_index("dp")
@@ -70,12 +84,6 @@
     y = (dp // NZ) % NY
     z = dp % NZ
 
-    def load(b, carry):
-        pltpu.make_async_copy(features.at[:, pl.ds(pl.multiple_of(b * B, B), B)], feat.at[b], feat_sem).start()
-        return carry
-
-    lax.fori_loop(0, OWNERS, load, 0)
-
     def at(xx, yy, zz, cc):
         return (dp_index(xx, yy, zz), cc)
 
@@ -88,22 +96,46 @@
     peers = [sibling] + xnb[1:] + ynb[1:] + znb[1:]
     for peer in peers:
         pl.semaphore_signal(barrier, inc=1, device_id=peer, device_id_type=MESH)
+    small = [
+        pltpu.make_async_copy(a, b, small_sem.at[i])
+        for i, (a, b) in enumerate(((damping_in, damping), (slab_in, slab_t)))
+    ]
+    for copy in small:
+        copy.start()
+
+    def load(b, carry):
+        pltpu.make_async_copy(features.at[:, pl.ds(pl.multiple_of(b * B, B), B)], feat.at[b], feat_sem).start()
+        return carry
+
+    lax.fori_loop(0, OWNERS, load, 0)
+
     def remote(src, dst, s, r, dev):
         return pltpu.make_async_remote_copy(
             src_ref=src, dst_ref=dst, send_sem=s, recv_sem=r, device_id=dev, device_id_type=MESH
         )
 
+    row = lax.broadcasted_iota(jnp.int32, (H, H), 0)
+    col = lax.broadcasted_iota(jnp.int32, (H, H), 1)
+    owners = jnp.broadcast_to(owner_of[...].astype(F32), (OWNERS, OWNERS)).T
+    held = jnp.where(owners == col.astype(F32), row, 0)
+    table[...] = jnp.minimum(jnp.sum(held, axis=0, keepdims=True), OWNERS - 1)
+    copy = pltpu.make_async_copy(table, slot_block, small_sem.at[2])
+    copy.start()
+    copy.wait()
     pltpu.make_async_copy(feat, feat, feat_sem).wait()
+    for copy in small:
+        copy.wait()
 
     def slot_of(dx, dy, k, cc):
         return dp_index((x + dx) % NX, (y + dy) % NY, 2 * k + cc)
 
     def block_of(dx, dy, k, cc):
-        return feat[slot_block[slot_of(dx, dy, k, cc)]]
+        return feat[slot_block[0, slot_of(dx, dy, k, cc)]]
 
     def stage(g, carry):
+        dx, dy = pick(g)
         for k in range(NK):
-            xs[g, k] = block_of(order(g // 4), order(g % 4), k, 1 - c)
+            xs[g, k] = block_of(dx, dy, k, 1 - c)
         return carry
 
     lax.fori_loop(0, 16, stage, 0)
@@ -113,10 +145,7 @@
         remote(xs.at[g], xr.at[g], ex_s.at[g], ex_r.at[g], sibling).start()
         return carry
 
-    lax.fori_loop(0, 16, exchange, 0)
-
-    row = lax.broadcasted_iota(jnp.int32, (H, H), 0)
-    col = lax.broadcasted_iota(jnp.int32, (H, H), 1)
+    lax.fori_loop(0, AHEAD, exchange, 0)
 
     def level1(kind, axis, way, t):
         dev = (xnb, ynb)[axis][1 if way == 0 else 3]
@@ -138,7 +167,12 @@
         level1(kind, part, way, t).start()
 
     def group(g, carry):
-        dx, dy = order(g // 4), order(g % 4)
+        dx, dy = pick(g)
+
+        @pl.when(g + AHEAD < 16)
+        def _():
+            exchange(g + AHEAD, 0)
+
         remote(xs.at[g], xr.at[g], ex_s.at[g], ex_r.at[g], sibling).wait_recv()
 
         for k in range(NK):
@@ -189,17 +223,31 @@
 
     lax.fori_loop(0, 4, pass_on, 0)
 
-    def add_coded(ref, part, half, coded, tokens):
+    def add_coded(ref, part, half, coded):
         for message in coded:
-            parts, rows = decode(message, tokens)
+            parts, rows = decode(message, 512)
             for k in range(NK):
                 ref[half, k, :HA] = ref[half, k, :HA] + parts[k]
                 if part == 1:
                     ref[half, k, HA:] = ref[half, k, HA:] + rows[k]
 
-    def level2(part, d):
+    def level2(part, d, pair):
         dev = at(x, (y + d) % NY, z, c) if part == 0 else at((x + d) % NX, y, z, c)
-        return remote(sent2.at[part, d], got2.at[part, d], l2_s.at[part, d], l2_r.at[part, d], dev)
+        return remote(
+            sent2.at[part, d, pair], got2.at[part, d, pair], l2_s.at[part, d, pair], l2_r.at[part, d, pair], dev
+        )
+
+    halves = [(half, n) for half in (0, 1) for n in (0, 1)]
+
+    def far(pair, n):
+        return ((z - c + NZ) // 2 + ((2, 3), (1, 0))[pair][n]) % NK
+
+    def send2(part, t, pair):
+        ref = place(part, 0, t)
+        parts = [ref[half, far(pair, n), :HA] for half, n in halves]
+        diagonals = {2 * half + n: ref[half, far(pair, n), HA : HA + 1] for half, n in halves} if part == 1 else {}
+        encode(sent2.at[part, t, pair], parts, diagonals, 1024)
+        level2(part, t, pair).start()
 
     def finish1(i, carry):
         t = order(i)
@@ -209,28 +257,27 @@
                 level1(2, part, way, t).wait_recv()
             ref = place(part, 0, t)
             for half in (0, 1):
-                add_coded(ref, part, half, (got1.at[2, part, half, t], got1.at[1, part, 1 - half, t]), 512)
+                add_coded(ref, part, half, (got1.at[2, part, half, t], got1.at[1, part, 1 - half, t]))
 
             @pl.when(t != 0)
             def _():
-                for half in (0, 1):
-                    encode(sent2.at[part, t, half], *pieces(ref, part, half), 1024)
-                level2(part, t).start()
+                send2(part, t, 0)
         return carry
 
     lax.fori_loop(0, 4, finish1, 0)
 
-    for part in (0, 1):
-        for d in (1, 3, 2):
-            level2(part, d).wait_recv()
-            for half in (0, 1):
-                add_coded(place(part, 0, 0), part, half, (got2.at[part, d, half],), 1024)
+    def second_pair(i, carry):
+        for part in (0, 1):
+            send2(part, order(i), 1)
+        return carry
+
+    lax.fori_loop(0, 3, second_pair, 0)
 
     def level3(k):
         d = (2 * k + c - z + NZ) % NZ
         return remote(sent3.at[k], got3.at[d], l3_ss.at[k], l3_rs.at[d], at(x, y, 2 * k + c, c))
 
-    def send3(k, carry):
+    def send3(k):
         @pl.when(2 * k + c != z)
         def _():
             parts = [pa[0, 0, 0, k], pa[0, 0, 1, k], pb[0, 0, 0, k, :HA], pb[0, 0, 1, k, :HA]]
@@ -238,16 +285,27 @@
             encode(sent3.at[k], parts, diagonals, 4096)
             level3(k).start()
 
-        return carry
-
-    lax.fori_loop(0, NK, send3, 0)
+    for pair in (0, 1):
+        for part in (0, 1):
+            ref = place(part, 0, 0)
+            for d in (1, 3, 2):
+                level2(part, d, pair).wait_recv()
+                parts, rows = decode(got2.at[part, d, pair], 1024)
+                for half, n in halves:
+                    k = far(pair, n)
+                    ref[half, k, :HA] = ref[half, k, :HA] + parts[2 * half + n]
+                    if part == 1:
+                        ref[half, k, HA:] = ref[half, k, HA:] + rows[2 * half + n]
+        for n in (0, 1):
+            send3(far(pair, n))
 
     owner = z % 2 == c
     xy = x * NY + y
     kz = z // 2
 
     def ag1(d):
-        return remote(gathered.at[c, xy, kz], gathered.at[c, xy, kz], ag1_s.at[d], ag1_r.at[kz], znb[d])
+        j = rank((z + d) % NZ, c, kz)
+        return remote(gathered.at[c, xy, 0], gathered.at[c, xy, j], ag1_s.at[d], ag1_r.at[j], znb[d])
 
     @pl.when(owner)
     def _():
@@ -262,7 +320,7 @@
         scale = 1.0 / TOTAL
         t01 = jnp.concatenate([t01a, t01b], axis=0) * scale
         both = jnp.concatenate([ba, bb], axis=0) * scale
-        damp = damping[slot_block[dp]]
+        damp = damping[slot_block[0, dp]]
         d0 = d0 * scale + damp
         d1 = d1 * scale + damp
         flip = both.T
@@ -285,59 +343,71 @@
 
         v = second(slab_t[...])
         result = 2.0 * v - second(times(v))
-        gathered[c, xy, kz] = result.astype(BF16)
-        for d in range(1, NZ):
+        gathered[c, xy, 0] = result.astype(BF16)
+        for d in (1, 7, 4, 3, 5, 2, 6):
             ag1(d).start()
 
-    for k in range(NK):
-        @pl.when(2 * k + c != z)
-        def _():
-            pltpu.make_async_remote_copy(
-                src_ref=gathered.at[c, xy, k], dst_ref=gathered.at[c, xy, k], send_sem=ag1_s.at[0], recv_sem=ag1_r.at[k],
-                device_id=sibling, device_id_type=MESH,
-            ).wait_recv()
-
-    def bundle(cc, h, q):
-        return gathered.at[cc, q, pl.ds(2 * h, 2)]
-
-    def line(h, d):
-        return x * NY + (y + d) % NY if h == 0 else ((x + d) % NX) * NY + y
-
-    def ag2(h, d):
-        dev = ynb[d] if h == 0 else xnb[d]
-        return remote(bundle(c, h, xy), bundle(c, h, xy), ag2_s.at[h, d], ag_r.at[h, xy], dev)
-
-    def ag3(h, e, d):
-        q = line(h, e)
-        dev = xnb[d] if h == 0 else ynb[d]
-        return remote(bundle(c, h, q), bundle(c, h, q), ag3_s.at[h, e, d], ag_r.at[h, q], dev)
-
-    def landed(h, q):
-        remote(bundle(c, h, q), bundle(c, h, q), ag2_s.at[0, 0], ag_r.at[h, q], sibling).wait_recv()
-
-    def forward(cc, h, q):
-        return remote(bundle(cc, h, q), bundle(cc, h, q), fw_s.at[h, q], fw_r.at[h, q], sibling)
-
-    for h in (0, 1):
+    def along(j, e, d):
+        ex, ey = (d, e) if j % 2 == 0 else (e, d)
+        return ((x + ex) % NX) * NY + (y + ey) % NY
+
+    def first_line(j):
+        return ynb if j % 2 == 0 else xnb
+
+    def last_line(j):
+        return xnb if j % 2 == 0 else ynb
+
+    def whole(j, q, s, r, dev):
+        return remote(gathered.at[c, q, j], gathered.at[c, q, j], s, r, dev)
+
+    def ag2(j, d):
+        return whole(j, xy, ag2_s.at[j, d], ag_r.at[j, xy], first_line(j)[d])
+
+    def ag3(j, e, d):
+        q = along(j, e, 0)
+        return whole(j, q, ag3_s.at[j, e, d], ag_r.at[j, q], last_line(j)[d])
+
+    def landed(j, q):
+        whole(j, q, ag2_s.at[0, 0], ag_r.at[j, q], sibling).wait_recv()
+
+    def forward(cc, j, q):
+        return remote(gathered.at[cc, q, j], gathered.at[cc, q, j], fw_s.at[j, q], fw_r.at[j, q], sibling)
+
+    def pass1(j):
+        def arrive():
+            whole(j, xy, ag1_s.at[0], ag1_r.at[j], sibling).wait_recv()
+
+        if j == 0:
+            pl.when(jnp.logical_not(owner))(arrive)
+        else:
+            arrive()
         for d in (2, 1, 3):
-            ag2(h, d).start()
-    for h in (0, 1):
+            ag2(j, d).start()
         for d in (2, 1, 3):
-            ag3(h, 0, d).start()
-        forward(c, h, xy).start()
-    for e in (1, 3, 2):
-        for h in (0, 1):
-            landed(h, line(h, e))
+            ag3(j, 0, d).start()
+        forward(c, j, xy).start()
+
+    def pass2(j):
+        for e in (1, 3, 2):
+            q = along(j, e, 0)
+            landed(j, q)
             for d in (2, 1, 3):
-                ag3(h, e, d).start()
-            forward(c, h, line(h, e)).start()
-    for e in (0, 1, 3, 2):
-        for d in (1, 3, 2):
-            for h in (0, 1):
-                ex, ey = (d, e) if h == 0 else (e, d)
-                q = ((x + ex) % NX) * NY + (y + ey) % NY
-                landed(h, q)
-                forward(c, h, q).start()
+                ag3(j, e, d).start()
+            forward(c, j, q).start()
+
+    def pass3(j):
+        for e in (0, 1, 3, 2):
+            for d in (1, 3, 2):
+                q = along(j, e, d)
+                landed(j, q)
+                forward(c, j, q).start()
+
+    for j in range(NK):
+        pass1(j)
+    for j in range(NK):
+        pass2(j)
+    for j in range(NK):
+        pass3(j)
 
     def sent_exchange(g, carry):
         remote(xs.at[g], xr.at[g], ex_s.at[g], ex_r.at[g], sibling).wait_send()
@@ -355,7 +425,8 @@
     lax.fori_loop(0, 4, sent_level1, 0)
     for part in (0, 1):
         for d in (1, 2, 3):
-            level2(part, d).wait_send()
+            for pair in (0, 1):
+                level2(part, d, pair).wait_send()
     for k in range(NK):
         @pl.when(2 * k + c != z)
         def _():
@@ -366,27 +437,32 @@
         for d in range(1, NZ):
             ag1(d).wait_send()
 
-    for h in (0, 1):
+    for j in range(NK):
         for d in (1, 2, 3):
-            ag2(h, d).wait_send()
+            ag2(j, d).wait_send()
             for e in range(4):
-                ag3(h, e, d).wait_send()
+                ag3(j, e, d).wait_send()
 
     def sent_forward(q, carry):
-        for h in (0, 1):
-            forward(c, h, q).wait_send()
-            forward(1 - c, h, q).wait_recv()
+        for j in range(NK):
+            forward(c, j, q).wait_send()
+            forward(1 - c, j, q).wait_recv()
         return carry
 
     lax.fori_loop(0, 16, sent_forward, 0)
 
 
 def permute_kernel(owner_of, gathered, out, sem):
+    here = lax.axis_index("dp") % NZ
+    nearest = [lax.shift_right_logical(here - plane + NZ, 1) & (NK - 1) for plane in (0, 1)]
+
     def one(b, carry):
         o = owner_of[b]
-        q, z = o // NZ, o % NZ
+        q, plane = lax.shift_right_logical(o, 3), o & 1
+        away = (lax.shift_right_logical(o, 1) - jnp.where(plane == 0, *nearest)) & (NK - 1)
+        j = away ^ lax.shift_right_logical(away, 1)
         pltpu.make_async_copy(
-            gathered.at[z % 2, q, z // 2], out.at[:, pl.ds(pl.multiple_of(b * B, B), B)], sem
+            gathered.at[plane, q, j], out.at[:, pl.ds(pl.multiple_of(b * B, B), B)], sem
         ).start()
         return carry
 
@@ -395,17 +471,19 @@
 
 
 def shards(features, grad_slab, damping, owner_of):
-    slots = jnp.arange(OWNERS, dtype=jnp.int32)
-    slot_block = jnp.sum(jnp.where(owner_of[None, :] == slots[:, None], slots[None, :], 0), axis=1)
     vmem = pl.BlockSpec(memory_space=pltpu.VMEM)
     smem = pl.BlockSpec(memory_space=pltpu.SMEM)
     dma = pltpu.SemaphoreType.DMA
     gathered = pl.pallas_call(
         reduce_kernel,
         out_shape=pltpu.VMEM((2, NX * NY, NK, COLS, B), BF16),
-        in_specs=[smem, smem, pl.BlockSpec(memory_space=pl.ANY), vmem],
+        in_specs=[vmem] + [pl.BlockSpec(memory_space=pl.ANY)] * 3,
         out_specs=vmem,
         scratch_shapes=[
+            pltpu.SMEM((1, OWNERS), jnp.int32),
+            pltpu.SMEM((OWNERS,), F32),
+            pltpu.VMEM((COLS, B), F32),
+            pltpu.VMEM((1, OWNERS), jnp.int32),
             pltpu.VMEM((OWNERS, ROWS, B), BF16),
             pltpu.VMEM((16, NK, ROWS, B), BF16),
             pltpu.VMEM((16, NK, ROWS, B), BF16),
@@ -417,19 +495,19 @@
             pltpu.VMEM((2, 4, 2, CODED, H), jnp.int16),
             pltpu.VMEM((NK, CODED, H), jnp.int16),
             pltpu.VMEM((NZ, CODED, H), jnp.int16),
-            dma,
+            dma((3,)), dma,
             dma((16,)), dma((16,)),
             dma((3, 2, 2, 4)), dma((3, 2, 2, 4)),
-            dma((2, 4)), dma((2, 4)),
+            dma((2, 4, 2)), dma((2, 4, 2)),
             dma((NK,)), dma((NZ,)),
             dma((NZ,)), dma((NK,)),
-            dma((2, 4)), dma((2, 4, 4)), dma((2, 16)),
-            dma((2, 16)), dma((2, 16)),
+            dma((NK, 4)), dma((NK, 4, 4)), dma((NK, 16)),
+            dma((NK, 16)), dma((NK, 16)),
         ],
         compiler_params=pltpu.CompilerParams(
             collective_id=0, has_side_effects=True, vmem_limit_bytes=58 * 1024 * 1024
         ),
-    )(slot_block, damping, features, grad_slab.T)
+    )(owner_of.reshape(1, OWNERS), damping, features, grad_slab.T)
     out = pl.pallas_call(
         permute_kernel,
         out_shape=jax.ShapeDtypeStruct((COLS, OWNERS * B), BF16),

time: 81.6 us -> 76.2 us (0.934)
  Pallas kernels: 80.1 us -> 76.1 us
  other arithmetic: 1.28 us -> 0 us
    pallas_call x1, Pallas kernels: 77.1 us -> 73.6 us  [shards(): pl.pallas_call(reduce_kernel, out_shape=pltpu.VMEM((2, NX * NY, NK, COLS,...]
    reduce_sum x1 -> x0, other arithmetic: 1.28 us -> none  [shards(): jnp.sum(jnp.where(owner_of[None, :] == slots[:, None], slots[None, :], 0)...]
where the time goes in v3:
time: 76.2 us; the launch traced here: 76.1 us
  Pallas kernels  76.1 us (100%)
    pallas_call x1, Pallas kernels, shards(): pl.pallas_call(reduce_kernel, out_shape=pltpu.VMEM((2, NX * NY, NK, COLS,...  73.6 us
    pallas_call x1, Pallas kernels, shards(): pl.pallas_call(permute_kernel, out_shape=jax.ShapeDtypeStruct((COLS, OWNE...  2.53 us

profile of v3, /device:TPU:1, one launch (start us, length us, event | category | flops | bytes accessed | tf_op | source)
XLA Modules:
  0.0 76.1 jit_solution(3892401207483263738)
XLA Ops:
  0.0 0.0 copy-start
  0.0 73.6 %shard_map.46.gathered = bf16[2,16,4,64,256]{4,3,2,1,0:T(8,128)(2,1)S(1)} custom-call(s32[1,128]{1,0:T(1,128)} %bitcast.3, f32[128]{0:T(128)} %damping_in.1, bf16[128,32768]{1,0:T(8,128)(2,1)} %features.1, f32[64,256]{1,0:T(8,128)} %bitcast.4), custom_call_target="tpu_custom_call" | custom-call | tf_op jit(solution)/shard_map/pallas_call | solution.py:477
  73.6 0.0 copy-done
  73.6 2.5 %shard_map.47 = bf16[64,32768]{1,0:T(8,128)(2,1)} custom-call(s32[128]{0:T(128)S(1)} %copy-done, bf16[2,16,4,64,256]{4,3,2,1,0:T(8,128)(2,1)S(1)} %shard_map.46.gathered), custom_call_target="tpu_custom_call" | custom-call | tf_op jit(solution)/shard_map/pallas_call | solution.py:511
Async XLA Ops:
  0.0 73.6 %copy-start = (s32[128]{0:T(128)S(1)}, s32[128]{0:T(128)}, u32[]{:S(2)}) copy-start(s32[128]{0:T(128)} %owner_of.1) | copy-start | bytes 1540

commit v4 on v3

--- a/solution.py
+++ b/solution.py
@@ -13,7 +13,7 @@
 NK = NZ // 2
 OWNERS = NX * NY * NZ
 ROWS = 128
-AHEAD = 3
+AHEAD = 5
 HA = 64
 HB = 72
 CODED = 4 * HA + 16
@@ -75,7 +75,7 @@
 def reduce_kernel(
     owner_of, damping_in, features, slab_in, gathered,
     slot_block, damping, slab_t, table, feat, xs, xr, pa, pb, sent1, got1, sent2, got2, sent3, got3,
-    small_sem, feat_sem, ex_s, ex_r, l1_s, l1_r, l2_s, l2_r, l3_ss, l3_rs,
+    turn, small_sem, feat_sem, ex_s, ex_r, l1_s, l1_r, l2_s, l2_r, l3_ss, l3_rs,
     ag1_s, ag1_r, ag2_s, ag3_s, ag_r, fw_s, fw_r,
 ):
     dp = lax.axis_index("dp")
@@ -138,7 +138,7 @@
             xs[g, k] = block_of(dx, dy, k, 1 - c)
         return carry
 
-    lax.fori_loop(0, 16, stage, 0)
+    lax.fori_loop(0, AHEAD, stage, 0)
     pl.semaphore_wait(barrier, len(peers))
 
     def exchange(g, carry):
@@ -164,13 +164,17 @@
     def send1(kind, part, d, half, way, t):
         parts, diagonals = pieces(place(part, d, t), part, half)
         encode(sent1.at[kind, part, way, t], parts, diagonals, 512)
-        level1(kind, part, way, t).start()
+
+        @pl.when(c == 0)
+        def _():
+            level1(kind, part, way, t).start()
 
     def group(g, carry):
         dx, dy = pick(g)
 
         @pl.when(g + AHEAD < 16)
         def _():
+            stage(g + AHEAD, 0)
             exchange(g + AHEAD, 0)
 
         remote(xs.at[g], xr.at[g], ex_s.at[g], ex_r.at[g], sibling).wait_recv()
@@ -208,6 +212,22 @@
 
     lax.fori_loop(0, 16, group, 0)
 
+    def each1(kinds, action):
+        def step(i, carry):
+            for kind in kinds:
+                for part in (0, 1):
+                    for way in (0, 1):
+                        action(level1(kind, part, way, order(i)))
+            return carry
+
+        lax.fori_loop(0, 4, step, 0)
+
+    @pl.when(c == 1)
+    def _():
+        pl.semaphore_wait(turn, 1)
+        each1((0,), lambda copy: copy.start())
+        each1((1,), lambda copy: copy.start())
+
     def pass_on(i, carry):
         t = order(i)
         for part in (0, 1):
@@ -265,6 +285,11 @@
         return carry
 
     lax.fori_loop(0, 4, finish1, 0)
+
+    @pl.when(c == 0)
+    def _():
+        each1((0, 1), lambda copy: copy.wait_send())
+        pl.semaphore_signal(turn, inc=1, device_id=sibling, device_id_type=MESH)
 
     def second_pair(i, carry):
         for part in (0, 1):
@@ -312,11 +337,12 @@
         t01a, t01b = pa[0, 0, 0, kz], pa[0, 0, 1, kz]
         ba, bb = pb[0, 0, 0, kz, :HA], pb[0, 0, 1, kz, :HA]
         d0, d1 = pb[0, 0, 0, kz, HA : HA + 1], pb[0, 0, 1, kz, HA : HA + 1]
-        for d in (1, 7, 2, 6, 3, 5, 4):
-            remote(got3.at[d], got3.at[d], l3_ss.at[0], l3_rs.at[d], znb[d]).wait_recv()
+        def arrive3(d, total):
+            remote(got3.at[d], got3.at[d], l3_ss.at[0], l3_rs.at[d], sibling).wait_recv()
             parts, rows = decode(got3.at[d], 4096)
-            t01a, t01b, ba, bb = t01a + parts[0], t01b + parts[1], ba + parts[2], bb + parts[3]
-            d0, d1 = d0 + rows[2], d1 + rows[3]
+            return tuple(a + b for a, b in zip(total, (*parts, rows[2], rows[3])))
+
+        t01a, t01b, ba, bb, d0, d1 = lax.fori_loop(1, NZ, arrive3, (t01a, t01b, ba, bb, d0, d1))
         scale = 1.0 / TOTAL
         t01 = jnp.concatenate([t01a, t01b], axis=0) * scale
         both = jnp.concatenate([ba, bb], axis=0) * scale
@@ -348,24 +374,18 @@
             ag1(d).start()
 
     def along(j, e, d):
-        ex, ey = (d, e) if j % 2 == 0 else (e, d)
-        return ((x + ex) % NX) * NY + (y + ey) % NY
-
-    def first_line(j):
-        return ynb if j % 2 == 0 else xnb
-
-    def last_line(j):
-        return xnb if j % 2 == 0 else ynb
+        even = j % 2 == 0
+        return ((x + jnp.where(even, d, e)) % NX) * NY + (y + jnp.where(even, e, d)) % NY
 
     def whole(j, q, s, r, dev):
         return remote(gathered.at[c, q, j], gathered.at[c, q, j], s, r, dev)
 
     def ag2(j, d):
-        return whole(j, xy, ag2_s.at[j, d], ag_r.at[j, xy], first_line(j)[d])
+        return whole(j, xy, ag2_s.at[j, d], ag_r.at[j, xy], (along(j, d, 0) * NZ + z, c))
 
     def ag3(j, e, d):
         q = along(j, e, 0)
-        return whole(j, q, ag3_s.at[j, e, d], ag_r.at[j, q], last_line(j)[d])
+        return whole(j, q, ag3_s.at[j, e, d], ag_r.at[j, q], (along(j, 0, d) * NZ + z, c))
 
     def landed(j, q):
         whole(j, q, ag2_s.at[0, 0], ag_r.at[j, q], sibling).wait_recv()
@@ -373,41 +393,38 @@
     def forward(cc, j, q):
         return remote(gathered.at[cc, q, j], gathered.at[cc, q, j], fw_s.at[j, q], fw_r.at[j, q], sibling)
 
-    def pass1(j):
-        def arrive():
+    def pass1(j, carry):
+        @pl.when(jnp.logical_or(j > 0, jnp.logical_not(owner)))
+        def _():
             whole(j, xy, ag1_s.at[0], ag1_r.at[j], sibling).wait_recv()
 
-        if j == 0:
-            pl.when(jnp.logical_not(owner))(arrive)
-        else:
-            arrive()
         for d in (2, 1, 3):
             ag2(j, d).start()
         for d in (2, 1, 3):
             ag3(j, 0, d).start()
         forward(c, j, xy).start()
-
-    def pass2(j):
-        for e in (1, 3, 2):
-            q = along(j, e, 0)
+        return carry
+
+    def pass2(i, carry):
+        j, e = i // 3, 2 * (i % 3) + 1 - 3 * ((i % 3) // 2)
+        q = along(j, e, 0)
+        landed(j, q)
+        for d in (2, 1, 3):
+            ag3(j, e, d).start()
+        forward(c, j, q).start()
+        return carry
+
+    def pass3(i, carry):
+        j, e = i // 4, i % 4
+        for d in (1, 3, 2):
+            q = along(j, e, d)
             landed(j, q)
-            for d in (2, 1, 3):
-                ag3(j, e, d).start()
             forward(c, j, q).start()
-
-    def pass3(j):
-        for e in (0, 1, 3, 2):
-            for d in (1, 3, 2):
-                q = along(j, e, d)
-                landed(j, q)
-                forward(c, j, q).start()
-
-    for j in range(NK):
-        pass1(j)
-    for j in range(NK):
-        pass2(j)
-    for j in range(NK):
-        pass3(j)
+        return carry
+
+    lax.fori_loop(0, NK, pass1, 0)
+    lax.fori_loop(0, 3 * NK, pass2, 0)
+    lax.fori_loop(0, 4 * NK, pass3, 0)
 
     def sent_exchange(g, carry):
         remote(xs.at[g], xr.at[g], ex_s.at[g], ex_r.at[g], sibling).wait_send()
@@ -415,14 +432,11 @@
 
     lax.fori_loop(0, 16, sent_exchange, 0)
 
-    def sent_level1(t, carry):
-        for kind in range(3):
-            for axis in (0, 1):
-                for way in (0, 1):
-                    level1(kind, axis, way, t).wait_send()
-        return carry
-
-    lax.fori_loop(0, 4, sent_level1, 0)
+    @pl.when(c == 1)
+    def _():
+        each1((0, 1), lambda copy: copy.wait_send())
+
+    each1((2,), lambda copy: copy.wait_send())
     for part in (0, 1):
         for d in (1, 2, 3):
             for pair in (0, 1):
@@ -437,11 +451,14 @@
         for d in range(1, NZ):
             ag1(d).wait_send()
 
-    for j in range(NK):
+    def sent_gather(j, carry):
         for d in (1, 2, 3):
             ag2(j, d).wait_send()
             for e in range(4):
                 ag3(j, e, d).wait_send()
+        return carry
+
+    lax.fori_loop(0, NK, sent_gather, 0)
 
     def sent_forward(q, carry):
         for j in range(NK):
@@ -495,7 +512,7 @@
             pltpu.VMEM((2, 4, 2, CODED, H), jnp.int16),
             pltpu.VMEM((NK, CODED, H), jnp.int16),
             pltpu.VMEM((NZ, CODED, H), jnp.int16),
-            dma((3,)), dma,
+            pltpu.SemaphoreType.REGULAR, dma((3,)), dma,
             dma((16,)), dma((16,)),
             dma((3, 2, 2, 4)), dma((3, 2, 2, 4)),
             dma((2, 4, 2)), dma((2, 4, 2)),

time: 76.2 us -> 73.2 us (0.961)
  Pallas kernels: 76.1 us -> 73.1 us
    pallas_call x1, Pallas kernels: 73.6 us -> 70.5 us  [shards(): pl.pallas_call(reduce_kernel, out_shape=pltpu.VMEM((2, NX * NY, NK, COLS,...]
where the time goes in v4:
time: 73.2 us; the launch traced here: 73.1 us
  Pallas kernels  73.1 us (100%)
    pallas_call x1, Pallas kernels, shards(): pl.pallas_call(reduce_kernel, out_shape=pltpu.VMEM((2, NX * NY, NK, COLS,...  70.5 us
    pallas_call x1, Pallas kernels, shards(): pl.pallas_call(permute_kernel, out_shape=jax.ShapeDtypeStruct((COLS, OWNE...  2.53 us

profile of v4, /device:TPU:1, one launch (start us, length us, event | category | flops | bytes accessed | tf_op | source)
XLA Modules:
  0.0 73.1 jit_solution(11678895094227517453)
XLA Ops:
  0.0 0.0 copy-start
  0.0 70.5 %shard_map.46.gathered = bf16[2,16,4,64,256]{4,3,2,1,0:T(8,128)(2,1)S(1)} custom-call(s32[1,128]{1,0:T(1,128)} %bitcast.3, f32[128]{0:T(128)} %damping_in.1, bf16[128,32768]{1,0:T(8,128)(2,1)} %features.1, f32[64,256]{1,0:T(8,128)} %bitcast.4), custom_call_target="tpu_custom_call" | custom-call | tf_op jit(solution)/shard_map/pallas_call | solution.py:494
  70.5 0.0 copy-done
  70.6 2.5 %shard_map.47 = bf16[64,32768]{1,0:T(8,128)(2,1)} custom-call(s32[128]{0:T(128)S(1)} %copy-done, bf16[2,16,4,64,256]{4,3,2,1,0:T(8,128)(2,1)S(1)} %shard_map.46.gathered), custom_call_target="tpu_custom_call" | custom-call | tf_op jit(solution)/shard_map/pallas_call | solution.py:528
Async XLA Ops:
  0.0 70.6 %copy-start = (s32[128]{0:T(128)S(1)}, s32[128]{0:T(128)}, u32[]{:S(2)}) copy-start(s32[128]{0:T(128)} %owner_of.1) | copy-start | bytes 1540

commit v5 on v4

--- a/solution.py
+++ b/solution.py
@@ -13,7 +13,7 @@
 NK = NZ // 2
 OWNERS = NX * NY * NZ
 ROWS = 128
-AHEAD = 5
+AHEAD = 8
 HA = 64
 HB = 72
 CODED = 4 * HA + 16
@@ -72,11 +72,18 @@
     return parts, [rows[i : i + 1] for i in range(4)]
 
 
+def thirds(v):
+    high = v.astype(BF16)
+    rest = v - high.astype(F32)
+    middle = rest.astype(BF16)
+    return high, middle, (rest - middle.astype(F32)).astype(BF16)
+
+
 def reduce_kernel(
     owner_of, damping_in, features, slab_in, gathered,
     slot_block, damping, slab_t, table, feat, xs, xr, pa, pb, sent1, got1, sent2, got2, sent3, got3,
     turn, small_sem, feat_sem, ex_s, ex_r, l1_s, l1_r, l2_s, l2_r, l3_ss, l3_rs,
-    ag1_s, ag1_r, ag2_s, ag3_s, ag_r, fw_s, fw_r,
+    ag1_s, ag1_r, ag_s, ag_r, fw_s, fw_r,
 ):
     dp = lax.axis_index("dp")
     c = lax.axis_index("group")
@@ -357,8 +364,15 @@
         )
         alpha = 1.0 / jnp.max(jnp.sum(jnp.abs(mat), axis=0, keepdims=True), axis=1, keepdims=True)
 
+        m1, m2, m3 = thirds(mat)
+
         def times(v):
-            return jnp.dot(v, mat, precision=lax.Precision.HIGHEST, preferred_element_type=F32)
+            v1, v2, v3 = thirds(v)
+            a = jnp.dot(jnp.concatenate([v1, v2, v3], axis=0), m1, preferred_element_type=F32)
+            b = jnp.dot(jnp.concatenate([v1, v2], axis=0), m2, preferred_element_type=F32)
+            e = jnp.dot(v1, m3, preferred_element_type=F32)
+            small = a[2 * COLS :] + b[COLS:] + e
+            return a[:COLS] + ((a[COLS : 2 * COLS] + b[:COLS]) + small)
 
         def first(v):
             return 2.0 * alpha * v - alpha * alpha * times(v)
@@ -372,59 +386,6 @@
         gathered[c, xy, 0] = result.astype(BF16)
         for d in (1, 7, 4, 3, 5, 2, 6):
             ag1(d).start()
-
-    def along(j, e, d):
-        even = j % 2 == 0
-        return ((x + jnp.where(even, d, e)) % NX) * NY + (y + jnp.where(even, e, d)) % NY
-
-    def whole(j, q, s, r, dev):
-        return remote(gathered.at[c, q, j], gathered.at[c, q, j], s, r, dev)
-
-    def ag2(j, d):
-        return whole(j, xy, ag2_s.at[j, d], ag_r.at[j, xy], (along(j, d, 0) * NZ + z, c))
-
-    def ag3(j, e, d):
-        q = along(j, e, 0)
-        return whole(j, q, ag3_s.at[j, e, d], ag_r.at[j, q], (along(j, 0, d) * NZ + z, c))
-
-    def landed(j, q):
-        whole(j, q, ag2_s.at[0, 0], ag_r.at[j, q], sibling).wait_recv()
-
-    def forward(cc, j, q):
-        return remote(gathered.at[cc, q, j], gathered.at[cc, q, j], fw_s.at[j, q], fw_r.at[j, q], sibling)
-
-    def pass1(j, carry):
-        @pl.when(jnp.logical_or(j > 0, jnp.logical_not(owner)))
-        def _():
-            whole(j, xy, ag1_s.at[0], ag1_r.at[j], sibling).wait_recv()
-
-        for d in (2, 1, 3):
-            ag2(j, d).start()
-        for d in (2, 1, 3):
-            ag3(j, 0, d).start()
-        forward(c, j, xy).start()
-        return carry
-
-    def pass2(i, carry):
-        j, e = i // 3, 2 * (i % 3) + 1 - 3 * ((i % 3) // 2)
-        q = along(j, e, 0)
-        landed(j, q)
-        for d in (2, 1, 3):
-            ag3(j, e, d).start()
-        forward(c, j, q).start()
-        return carry
-
-    def pass3(i, carry):
-        j, e = i // 4, i % 4
-        for d in (1, 3, 2):
-            q = along(j, e, d)
-            landed(j, q)
-            forward(c, j, q).start()
-        return carry
-
-    lax.fori_loop(0, NK, pass1, 0)
-    lax.fori_loop(0, 3 * NK, pass2, 0)
-    lax.fori_loop(0, 4 * NK, pass3, 0)
 
     def sent_exchange(g, carry):
         remote(xs.at[g], xr.at[g], ex_s.at[g], ex_r.at[g], sibling).wait_send()
@@ -446,27 +407,68 @@
         def _():
             level3(k).wait_send()
 
+    def along(j, e, d):
+        even = j % 2 == 0
+        return ((x + jnp.where(even, d, e)) % NX) * NY + (y + jnp.where(even, e, d)) % NY
+
+    def whole(j, q, s, r, dev):
+        return remote(gathered.at[c, q, j], gathered.at[c, q, j], s, r, dev)
+
+    def ag2(j, d):
+        return whole(j, xy, ag_s, ag_r.at[j, xy], (along(j, d, 0) * NZ + z, c))
+
+    def ag3(j, e, d):
+        q = along(j, e, 0)
+        return whole(j, q, ag_s, ag_r.at[j, q], (along(j, 0, d) * NZ + z, c))
+
+    def landed(j, q):
+        whole(j, q, ag_s, ag_r.at[j, q], sibling).wait_recv()
+
+    def forward(cc, j, q):
+        return remote(gathered.at[cc, q, j], gathered.at[cc, q, j], fw_s, fw_r, sibling)
+
+    def pass1(j, carry):
+        @pl.when(jnp.logical_or(j > 0, jnp.logical_not(owner)))
+        def _():
+            whole(j, xy, ag1_s.at[0], ag1_r.at[j], sibling).wait_recv()
+
+        for d in (2, 1, 3):
+            ag2(j, d).start()
+        for d in (2, 1, 3):
+            ag3(j, 0, d).start()
+        forward(c, j, xy).start()
+        return carry
+
+    def pass2(i, carry):
+        j, e = i // 3, 2 * (i % 3) + 1 - 3 * ((i % 3) // 2)
+        q = along(j, e, 0)
+        landed(j, q)
+        for d in (2, 1, 3):
+            ag3(j, e, d).start()
+        forward(c, j, q).start()
+        return carry
+
+    def pass3(i, carry):
+        j, e = i // 4, i % 4
+        for d in (1, 3, 2):
+            q = along(j, e, d)
+            landed(j, q)
+            forward(c, j, q).start()
+        return carry
+
+    lax.fori_loop(0, NK, pass1, 0)
+    lax.fori_loop(0, 3 * NK, pass2, 0)
+    lax.fori_loop(0, 4 * NK, pass3, 0)
+
     @pl.when(owner)
     def _():
         for d in range(1, NZ):
             ag1(d).wait_send()
 
-    def sent_gather(j, carry):
-        for d in (1, 2, 3):
-            ag2(j, d).wait_send()
-            for e in range(4):
-                ag3(j, e, d).wait_send()
-        return carry
-
-    lax.fori_loop(0, NK, sent_gather, 0)
-
-    def sent_forward(q, carry):
-        for j in range(NK):
-            forward(c, j, q).wait_send()
-            forward(1 - c, j, q).wait_recv()
-        return carry
-
-    lax.fori_loop(0, 16, sent_forward, 0)
+    most = gathered.at[c, pl.ds(0, 15)]
+    remote(most, most, ag_s, ag_r.at[0, 0], sibling).wait_send()
+    remote(gathered.at[c], gathered.at[c], fw_s, fw_r, sibling).wait_send()
+    remote(gathered.at[1 - c], gathered.at[1 - c], fw_s, fw_r, sibling).wait_recv()
 
 
 def permute_kernel(owner_of, gathered, out, sem):
@@ -518,8 +520,7 @@
             dma((2, 4, 2)), dma((2, 4, 2)),
             dma((NK,)), dma((NZ,)),
             dma((NZ,)), dma((NK,)),
-            dma((NK, 4)), dma((NK, 4, 4)), dma((NK, 16)),
-            dma((NK, 16)), dma((NK, 16)),
+            dma, dma((NK, 16)), dma, dma,
         ],
         compiler_params=pltpu.CompilerParams(
             collective_id=0, has_side_effects=True, vmem_limit_bytes=58 * 1024 * 1024

time: 73.2 us -> 70.6 us (0.964)
  Pallas kernels: 73.1 us -> 70.5 us
    pallas_call x1, Pallas kernels: 70.5 us -> 68 us  [shards(): pl.pallas_call(reduce_kernel, out_shape=pltpu.VMEM((2, NX * NY, NK, COLS,...]
where the time goes in v5:
time: 70.6 us; the launch traced here: 70.5 us
  Pallas kernels  70.5 us (100%)
    pallas_call x1, Pallas kernels, shards(): pl.pallas_call(reduce_kernel, out_shape=pltpu.VMEM((2, NX * NY, NK, COLS,...  68 us
    pallas_call x1, Pallas kernels, shards(): pl.pallas_call(permute_kernel, out_shape=jax.ShapeDtypeStruct((COLS, OWNE...  2.53 us

profile of v5, /device:TPU:1, one launch (start us, length us, event | category | flops | bytes accessed | tf_op | source)
XLA Modules:
  0.0 70.5 jit_solution(12031562005354780682)
XLA Ops:
  0.0 0.0 copy-start
  0.0 68.0 %shard_map.46.gathered = bf16[2,16,4,64,256]{4,3,2,1,0:T(8,128)(2,1)S(1)} custom-call(s32[1,128]{1,0:T(1,128)} %bitcast.3, f32[128]{0:T(128)} %damping_in.1, bf16[128,32768]{1,0:T(8,128)(2,1)} %features.1, f32[64,256]{1,0:T(8,128)} %bitcast.4), custom_call_target="tpu_custom_call" | custom-call | tf_op jit(solution)/shard_map/pallas_call | solution.py:496
  68.0 0.0 copy-done
  68.0 2.5 %shard_map.47 = bf16[64,32768]{1,0:T(8,128)(2,1)} custom-call(s32[128]{0:T(128)S(1)} %copy-done, bf16[2,16,4,64,256]{4,3,2,1,0:T(8,128)(2,1)S(1)} %shard_map.46.gathered), custom_call_target="tpu_custom_call" | custom-call | tf_op jit(solution)/shard_map/pallas_call | solution.py:529
Async XLA Ops:
  0.0 68.0 %copy-start = (s32[128]{0:T(128)S(1)}, s32[128]{0:T(128)}, u32[]{:S(2)}) copy-start(s32[128]{0:T(128)} %owner_of.1) | copy-start | bytes 1540

commit v6 on v5

--- a/solution.py
+++ b/solution.py
@@ -449,16 +449,21 @@
         return carry
 
     def pass3(i, carry):
-        j, e = i // 4, i % 4
         for d in (1, 3, 2):
-            q = along(j, e, d)
-            landed(j, q)
-            forward(c, j, q).start()
+            for e in (0, 1, 3, 2):
+                landed(2 * i, along(2 * i, e, d))
+            rows = gathered.at[c, pl.ds((x + d) % NX * NY, NY), 2 * i]
+            remote(rows, rows, fw_s, fw_r, sibling).start()
+        for e in (0, 1, 3, 2):
+            for d in (1, 3, 2):
+                q = along(2 * i + 1, e, d)
+                landed(2 * i + 1, q)
+                forward(c, 2 * i + 1, q).start()
         return carry
 
     lax.fori_loop(0, NK, pass1, 0)
     lax.fori_loop(0, 3 * NK, pass2, 0)
-    lax.fori_loop(0, 4 * NK, pass3, 0)
+    lax.fori_loop(0, NK // 2, pass3, 0)
 
     @pl.when(owner)
     def _():

time: 70.6 us -> 70.6 us (level)
  no operation moved by 1% of the time
where the time goes in v6:
time: 70.6 us; the launch traced here: 70.5 us
  Pallas kernels  70.5 us (100%)
    pallas_call x1, Pallas kernels, shards(): pl.pallas_call(reduce_kernel, out_shape=pltpu.VMEM((2, NX * NY, NK, COLS,...  68 us
    pallas_call x1, Pallas kernels, shards(): pl.pallas_call(permute_kernel, out_shape=jax.ShapeDtypeStruct((COLS, OWNE...  2.53 us

profile of v6, /device:TPU:1, one launch (start us, length us, event | category | flops | bytes accessed | tf_op | source)
XLA Modules:
  0.0 70.5 jit_solution(17619410762168097891)
XLA Ops:
  0.0 0.0 copy-start
  0.0 68.0 %shard_map.46.gathered = bf16[2,16,4,64,256]{4,3,2,1,0:T(8,128)(2,1)S(1)} custom-call(s32[1,128]{1,0:T(1,128)} %bitcast.3, f32[128]{0:T(128)} %damping_in.1, bf16[128,32768]{1,0:T(8,128)(2,1)} %features.1, f32[64,256]{1,0:T(8,128)} %bitcast.4), custom_call_target="tpu_custom_call" | custom-call | tf_op jit(solution)/shard_map/pallas_call | solution.py:501
  68.0 0.0 copy-done
  68.0 2.5 %shard_map.47 = bf16[64,32768]{1,0:T(8,128)(2,1)} custom-call(s32[128]{0:T(128)S(1)} %copy-done, bf16[2,16,4,64,256]{4,3,2,1,0:T(8,128)(2,1)S(1)} %shard_map.46.gathered), custom_call_target="tpu_custom_call" | custom-call | tf_op jit(solution)/shard_map/pallas_call | solution.py:534
Async XLA Ops:
  0.0 68.0 %copy-start = (s32[128]{0:T(128)S(1)}, s32[128]{0:T(128)}, u32[]{:S(2)}) copy-start(s32[128]{0:T(128)} %owner_of.1) | copy-start | bytes 1540
